TPU v7x, 128 devices: a whole 4x4x4 slice. The times are simulated.
128 devices in a mesh: tm: 16 (over x, z_lo, core), height: 4 (over y), mp: 2 (over z_hi).
Axes of the slice: x: 4, y: 4, z: 4 (z_hi: 2, z_lo: 2; z = z_hi * 2 + z_lo), core: 2. Of those that a mesh axis runs over, the one named last changes fastest.
Arguments:
- tokens: bfloat16 [32, 8, 48, 3072], P('tm', 'height'), may hold values from -60 to 60
- tangent: bfloat16 [32, 8, 48, 3072], P('tm', 'height'), may hold values from -6 to 6
- qkv_weight: bfloat16 [3072, 3, 1536], P('tm', None, 'mp'), may hold values from -0.109375 to 0.109375
- out_weight: bfloat16 [1536, 3072], P('mp', 'tm'), may hold values from -0.15625 to 0.15625
- reach: int32 [2, 12], P(None, 'mp'), may hold values from 0 to 1
Outputs:
- result: bfloat16 [32, 8, 48, 3072], P('tm', 'height', None, 'mp')
- result_tangent: bfloat16 [32, 8, 48, 3072], P('tm', 'height', None, 'mp')
All inputs are finite; a program needn't handle non-finite values.
Results may differ from a plain program's by a relative error of at most 0.024.
The roundings to bfloat16 on the way count: a program that leaves them out, or rounds other values in their place, can miss the bound.
Values may be sent and summed in bfloat16 or wider, within the bound.
A program may use at most 128 MiB of HBM per device.

v0:
```python
import jax
import jax.numpy as jnp
from jax import lax
from jax.sharding import PartitionSpec as P

D = 3072
DH = 128


def extended_2(cells, sides, width):
    for axis, dim in sides:
        count = lax.axis_size(axis)
        ends = count - 1
        head = lax.slice_in_dim(cells, 0, width, axis=dim)
        tail = lax.slice_in_dim(cells, cells.shape[dim] - width, cells.shape[dim], axis=dim)
        cells = jnp.concatenate(
            [
                lax.ppermute(tail, axis, [(i, (i + 1) % count) for i in range(ends)]),
                cells,
                lax.ppermute(head, axis, [((i + 1) % count, i) for i in range(ends)]),
            ],
            axis=dim,
        )
    return cells


def attend(query, query_move, key, key_move, value, value_move, allow):
    factor = 1.0 / query.shape[-1] ** 0.5
    scores = jnp.dot(query, key.T, preferred_element_type=jnp.float32) * factor
    slope = (
        jnp.dot(query_move, key.T, preferred_element_type=jnp.float32)
        + jnp.dot(query, key_move.T, preferred_element_type=jnp.float32)
    ) * factor
    scores = jnp.where(allow[None, :], scores, jnp.float32(-1e30))
    top = jnp.max(scores, axis=-1, keepdims=True)
    weights = jnp.where(allow[None, :], jnp.exp(scores - top), jnp.float32(0.0))
    probs = weights / jnp.sum(weights, axis=-1, keepdims=True)
    probs_low = probs.astype(jnp.bfloat16)
    output = jnp.dot(probs_low, value, preferred_element_type=jnp.float32)
    moved = probs * slope
    shift = jnp.sum(moved, axis=-1, keepdims=True)
    output_move = (
        jnp.dot(probs_low, value_move, preferred_element_type=jnp.float32)
        + jnp.dot(moved.astype(jnp.bfloat16), value, preferred_element_type=jnp.float32)
        - output * shift
    )
    return (output.astype(jnp.bfloat16), output_move.astype(jnp.bfloat16))


def per_device(tokens, tangent, qkv_weight, out_weight, reach):
    side, _, columns, width = tokens.shape
    tile_rows = side * side * columns
    local_width = qkv_weight.shape[2]
    heads_here = local_width // DH
    stacked = jnp.concatenate(
        [tokens.reshape(tile_rows, width), tangent.reshape(tile_rows, width)], 0
    )
    piece = lax.all_gather(qkv_weight, "tm", axis=0, tiled=True)
    projected = jnp.dot(
        stacked, piece.reshape(piece.shape[0], 3 * local_width), preferred_element_type=jnp.float32
    ).astype(jnp.bfloat16)
    projected = projected.reshape(2, side, side, columns, 3, local_width)
    packed = jnp.concatenate(
        [
            projected[0, :, :, :, 1],
            projected[0, :, :, :, 2],
            projected[1, :, :, :, 1],
            projected[1, :, :, :, 2],
        ],
        -1,
    )
    extended = extended_2(packed, (("tm", 0), ("height", 1)), side)
    key_values = jnp.transpose(extended.reshape(9 * tile_rows, 4, heads_here, DH), (1, 2, 0, 3))
    queries = jnp.transpose(
        projected[:, :, :, :, 0].reshape(2, tile_rows, heads_here, DH), (0, 2, 1, 3)
    )
    block = jnp.arange(3 * side) // side - 1
    frame_tile = lax.axis_index("tm")
    row_tile = lax.axis_index("height")
    frame_ok = (frame_tile + block >= 0) & (frame_tile + block < lax.axis_size("tm"))
    row_ok = (row_tile + block >= 0) & (row_tile + block < lax.axis_size("height"))
    allow_frames = (jnp.abs(block)[None, :] <= reach[0][:, None]) & frame_ok[None, :]
    allow_rows = (jnp.abs(block)[None, :] <= reach[1][:, None]) & row_ok[None, :]
    allow = allow_frames[:, :, None, None] & allow_rows[:, None, :, None]
    allow = jnp.broadcast_to(allow, (heads_here, 3 * side, 3 * side, columns)).reshape(
        heads_here, 9 * tile_rows
    )
    output, output_move = lax.map(
        lambda items: attend(*items),
        (queries[0], queries[1], key_values[0], key_values[2], key_values[1], key_values[3], allow),
    )
    hidden = jnp.concatenate(
        [
            jnp.transpose(output, (1, 0, 2)).reshape(tile_rows, local_width),
            jnp.transpose(output_move, (1, 0, 2)).reshape(tile_rows, local_width),
        ],
        0,
    )
    share = D // lax.axis_size("mp")
    lowest = lax.axis_index("mp") * share
    terms = jnp.dot(
        hidden,
        lax.all_gather(out_weight, "tm", axis=1, tiled=True),
        preferred_element_type=jnp.float32,
    )
    summed = lax.psum(terms, "mp")
    mixed = lax.dynamic_slice_in_dim(summed, lowest, share, 1)
    mixed = mixed.astype(jnp.bfloat16)
    result = mixed[:tile_rows].reshape(side, side, columns, -1)
    result_tangent = mixed[tile_rows:].reshape(side, side, columns, -1)
    return (result, result_tangent)


def solution(mesh):
    in_specs = (
        P("tm", "height", None, None),
        P("tm", "height", None, None),
        P("tm", None, "mp"),
        P("mp", "tm"),
        P(None, "mp"),
    )
    out_specs = (P("tm", "height", None, "mp"), P("tm", "height", None, "mp"))
    return jax.shard_map(
        per_device, mesh=mesh, in_specs=in_specs, out_specs=out_specs, check_vma=False
    )
```

profile of v0, /device:TPU:7, one launch (start us, length us, event | category | flops | bytes accessed | tf_op | source)
XLA Modules:
  0.0 450.4 jit_solution(4962050182728900433)
XLA Ops:
  8.0 83.6 %all-gather.3.cloned.1.call-done = bf16[3072,3,768]{2,0,1:T(8,128)(2,1)} async-done(((bf16[192,3,768]{2,0,1:T(8,128)(2,1)}), bf16[3072,3,768]{2,0,1:T(8,128)(2,1)}) %all-gather.3.cloned.1.call-update) | async-done | bytes 14155792 | tf_op jit(solution)/shard_map/all_gather | solution.py:58
  91.6 18.6 %copy.49 = bf16[3072,3,768]{0,2,1:T(8,128)(2,1)} copy(bf16[3072,3,768]{2,0,1:T(8,128)(2,1)} %all-gather.3.cloned.1.call-done) | data formatting | bytes 28311552 | tf_op jit(solution)/shard_map/all_gather | solution.py:58
  110.2 10.3 %convolution_convert_fusion = bf16[384,2304]{1,0:T(8,128)(2,1)} fusion(bf16[3072,2304]{0,1:T(8,128)(2,1)} %bitcast.115, bf16[192,3072]{1,0:T(8,128)(2,1)S(1)} %bitcast.119, bf16[192,3072]{1,0:T(8,128)(2,1)S(1)} %bitcast.120), kind=kOutput, calls=%fused_computation.46 | convolution fusion | flops 5441421312 | bytes 18284544 | tf_op jit(solution)/shard_map/dot_general | solution.py:59
  120.5 3.4 reshape.159
  124.0 2.5 fusion.54
  126.8 2.8 collective-permute-start
  129.6 1.9 collective-permute-start.1
  131.5 11.2 %collective-permute-done = bf16[2,2,48,3072]{3,2,1,0:T(8,128)(2,1)S(1)} collective-permute-done((bf16[2,2,48,3072]{3,2,1,0:T(8,128)(2,1)S(1)}, bf16[2,2,48,3072]{3,2,1,0:T(8,128)(2,1)S(1)}, u32[]{:S(2)}, u32[]{:S(2)}) %collective-permute-start) | collective-permute-done | bytes 1179680 | tf_op jit(solution)/shard_map/ppermute | solution.py:18
  142.7 14.9 %collective-permute-done.1 = bf16[2,2,48,3072]{3,2,1,0:T(8,128)(2,1)S(1)} collective-permute-done((bf16[2,2,48,3072]{3,2,1,0:T(8,128)(2,1)S(1)}, bf16[2,2,48,3072]{3,2,1,0:T(8,128)(2,1)S(1)}, u32[]{:S(2)}, u32[]{:S(2)}) %collective-permute-start.1) | collective-permute-done | bytes 1179680 | tf_op jit(solution)/shard_map/ppermute | solution.py:20
  157.6 2.1 pad_maximum_fusion.1
  159.7 5.3 %collective-permute-start.2 = (bf16[6,2,48,3072]{3,2,1,0:T(8,128)(2,1)}, bf16[6,2,48,3072]{3,2,1,0:T(8,128)(2,1)}, u32[]{:S(2)}, u32[]{:S(2)}) collective-permute-start(bf16[6,2,48,3072]{3,2,1,0:T(8,128)(2,1)} %pad_maximum_fusion.1), channel_id=1, source_target_pairs={{0,2},{2,4},{4,6},{1,3},{3,5},{5,7},{8,10},{10,12},{12,14},{9,11},... | collective-permute-start | bytes 10616840 | tf_op jit(solution)/shard_map/ppermute | solution.py:18
  168.2 3.9 slice_reduce_fusion
  172.2 2.8 reshape_squeeze.3
  177.7 52.1 %collective-permute-done.2 = bf16[6,2,48,3072]{3,2,1,0:T(8,128)(2,1)} collective-permute-done((bf16[6,2,48,3072]{3,2,1,0:T(8,128)(2,1)}, bf16[6,2,48,3072]{3,2,1,0:T(8,128)(2,1)}, u32[]{:S(2)}, u32[]{:S(2)}) %collective-permute-start.2) | collective-permute-done | bytes 3538976 | tf_op jit(solution)/shard_map/ppermute | solution.py:18
  229.8 5.9 %collective-permute-done.3 = bf16[6,2,48,3072]{3,2,1,0:T(8,128)(2,1)} collective-permute-done((bf16[6,2,48,3072]{3,2,1,0:T(8,128)(2,1)}, bf16[6,2,48,3072]{3,2,1,0:T(8,128)(2,1)}, u32[]{:S(2)}, u32[]{:S(2)}) %collective-permute-start.3) | collective-permute-done | bytes 3538976 | tf_op jit(solution)/shard_map/ppermute | solution.py:20
  235.7 8.1 %pad_maximum_fusion = bf16[6,6,48,3072]{3,2,1,0:T(8,128)(2,1)} fusion(bf16[6,2,48,3072]{3,2,1,0:T(8,128)(2,1)} %collective-permute-done.3, bf16[2,2,48,3072]{3,2,1,0:T(8,128)(2,1)S(1)} %copy-done.1, bf16[2,2,48,768]{3,2,1,0:T(8,128)(2,1)S(1)} %copy-done.7, bf16[2,2,48,768]{3,2,1,0:T(8,128)(2,1)S(1)} %copy-done.9, bf16[2,2,48,768]{3,2,1,0:T(8,128)(2,1)S(1)} %copy-done.3, ...), kind=kLoop, calls=%fused_computation.45 | loop fusion | flops 84934656 | bytes 21233664 | tf_op jit(solution)/shard_map/concatenate | solution.py:16
  243.9 21.9 %reshape.160 = bf16[1728,4,6,128]{3,2,1,0:T(8,128)(2,1)} reshape(bf16[6,6,48,3072]{3,2,1,0:T(8,128)(2,1)} %pad_maximum_fusion) | data formatting | bytes 21233664 | tf_op jit(solution)/shard_map/reshape | solution.py:73
  265.7 6.4 %slice_bitcast_fusion = (bf16[6,1728,128]{2,0,1:T(8,128)(2,1)S(1)}, bf16[6,1728,128]{2,0,1:T(8,128)(2,1)S(1)}, bf16[6,1728,128]{2,0,1:T(8,128)(2,1)S(1)}, bf16[6,1728,128]{2,0,1:T(8,128)(2,1)S(1)}) fusion(bf16[4,6,1728,128]{3,1,0,2:T(8,128)(2,1)} %bitcast.114), kind=kLoop, calls=%fused_computation.47 | loop fusion | bytes 21233664 | tf_op jit(solution)/shard_map/squeeze | solution.py:90
  272.5 1.9 copy.52
  274.4 1.9 copy.53
  276.3 1.8 copy.55
  278.1 53.8 %while.12 = (s32[]{:T(128)}, bf16[6,192,128]{2,1,0:T(8,128)(2,1)S(1)}, bf16[6,192,128]{2,1,0:T(8,128)(2,1)S(1)}, pred[6,1728]{1,0:T(8,128)(4,1)S(1)}, bf16[6,192...) while((s32[]{:T(128)}, ...), condition=%wide.region_4.5_spmd, body=%wide.region_0.4_spmd.sunk | while | flops 517029312 | bytes 14011441 | solution.py:88
  281.0 1.7 fusion.83
  289.9 1.7 fusion.83
  298.9 1.7 fusion.83
  307.9 1.7 fusion.83
  316.9 1.7 fusion.83
  320.1 1.5 bitcast_dynamic-update-slice_fusion.2
  325.8 1.7 fusion.83
  329.1 1.5 bitcast_dynamic-update-slice_fusion.2
  332.1 6.5 %fusion.44 = f32[384,3072]{1,0:T(8,128)} fusion(bf16[768,3072]{0,1:T(8,128)(2,1)} %all-gather.5.cloned.1.call-done, bf16[192,768]{1,0:T(8,128)(2,1)S(1)} %copy_bitcast_fusion, bf16[192,768]{1,0:T(8,128)(2,1)S(1)} %copy_bitcast_fusion.1), kind=kOutput, calls=%fused_computation.58 | convolution fusion | flops 1813118976 | bytes 10027008 | tf_op jit(solution)/shard_map/dot_general | solution.py:101
  338.6 103.8 %all-reduce.1 = bf16[384,3072]{1,0:T(8,128)(2,1)S(1)} all-reduce(f32[384,3072]{1,0:T(8,128)} %fusion.44), channel_id=1, replica_groups=mesh['tm'=16,'height'=4,'mp'=2] {'mp'}, use_global_device_ids=true, to_apply=%region_5.6 | all-reduce | flops 1179648 | bytes 7077888 | tf_op jit(solution)/shard_map/psum | solution.py:106
  (96 shorter events, 48.8 us)
Async XLA Ops:
  7.2 84.4 %all-gather.3.cloned.1.call-start = ((), (), s32[]{:S(2)}) async-start(), calls=%async_computation | async-start | bytes 15040512 | tf_op jit(solution)/shard_map/all_gather | solution.py:58
  7.9 102.3 %copy-start.13 = (bf16[2,2,48,3072]{3,2,1,0:T(8,128)(2,1)S(1)}, bf16[2,2,48,3072]{3,2,1,0:T(8,128)(2,1)}, u32[]{:S(2)}) copy-start(bf16[2,2,48,3072]{3,2,1,0:T(8,128)(2,1)} %param.8) | copy-start | bytes 3538948
  7.9 102.3 %copy-start.14 = (bf16[2,2,48,3072]{3,2,1,0:T(8,128)(2,1)S(1)}, bf16[2,2,48,3072]{3,2,1,0:T(8,128)(2,1)}, u32[]{:S(2)}) copy-start(bf16[2,2,48,3072]{3,2,1,0:T(8,128)(2,1)} %param.7) | copy-start | bytes 3538948
  7.9 324.2 %all-gather.5.cloned.1.call-start = ((), (), s32[]{:S(2)}) async-start(), calls=%async_computation.1 | async-start | bytes 5013504 | tf_op jit(solution)/shard_map/all_gather | solution.py:103
  126.5 33.2 %copy-start.2 = (bf16[2,2,48,768]{3,2,1,0:T(8,128)(2,1)}, bf16[2,2,48,768]{3,2,1,0:T(8,128)(2,1)S(1)}, u32[]{:S(2)}) copy-start(bf16[2,2,48,768]{3,2,1,0:T(8,128)(2,1)S(1)} %get-tuple-element.153) | copy-start | bytes 884740
  126.5 33.2 %copy-start.4 = (bf16[2,2,48,768]{3,2,1,0:T(8,128)(2,1)}, bf16[2,2,48,768]{3,2,1,0:T(8,128)(2,1)S(1)}, u32[]{:S(2)}) copy-start(bf16[2,2,48,768]{3,2,1,0:T(8,128)(2,1)S(1)} %get-tuple-element.154) | copy-start | bytes 884740
  126.6 33.1 %copy-start.6 = (bf16[2,2,48,768]{3,2,1,0:T(8,128)(2,1)}, bf16[2,2,48,768]{3,2,1,0:T(8,128)(2,1)S(1)}, u32[]{:S(2)}) copy-start(bf16[2,2,48,768]{3,2,1,0:T(8,128)(2,1)S(1)} %get-tuple-element.151) | copy-start | bytes 884740
  126.6 33.1 %copy-start.8 = (bf16[2,2,48,768]{3,2,1,0:T(8,128)(2,1)}, bf16[2,2,48,768]{3,2,1,0:T(8,128)(2,1)S(1)}, u32[]{:S(2)}) copy-start(bf16[2,2,48,768]{3,2,1,0:T(8,128)(2,1)S(1)} %get-tuple-element.152) | copy-start | bytes 884740
  126.8 39.6 %copy-start.12 = (s32[2,6]{1,0:T(2,128)S(1)}, s32[2,6]{1,0:T(2,128)}, u32[]{:S(2)}) copy-start(s32[2,6]{1,0:T(2,128)} %param.11) | copy-start | bytes 148
  126.8 15.9 %collective-permute-start = (bf16[2,2,48,3072]{3,2,1,0:T(8,128)(2,1)S(1)}, bf16[2,2,48,3072]{3,2,1,0:T(8,128)(2,1)S(1)}, u32[]{:S(2)}, u32[]{:S(2)}) collective-permute-start(bf16[2,2,48,3072]{3,2,1,0:T(8,128)(2,1)S(1)} %pad_maximum_fusion.2), channel_id=1, source_target_pairs={{0,8},{8,16},{16,24},{24,32},{32,40},{40,48},{48,56},{56,64},{64,7... | collective-permute-start | bytes 3538952 | tf_op jit(solution)/shard_map/ppermute | solution.py:18
  129.6 28.0 %collective-permute-start.1 = (bf16[2,2,48,3072]{3,2,1,0:T(8,128)(2,1)S(1)}, bf16[2,2,48,3072]{3,2,1,0:T(8,128)(2,1)S(1)}, u32[]{:S(2)}, u32[]{:S(2)}) collective-permute-start(bf16[2,2,48,3072]{3,2,1,0:T(8,128)(2,1)S(1)} %pad_maximum_fusion.2), channel_id=1, source_target_pairs={{8,0},{16,8},{24,16},{32,24},{40,32},{48,40},{56,48},{64,56},{72,6... | collective-permute-start | bytes 3538952 | tf_op jit(solution)/shard_map/ppermute | solution.py:20
  157.6 2.2 copy-start
  159.7 70.1 %collective-permute-start.2 = (bf16[6,2,48,3072]{3,2,1,0:T(8,128)(2,1)}, bf16[6,2,48,3072]{3,2,1,0:T(8,128)(2,1)}, u32[]{:S(2)}, u32[]{:S(2)}) collective-permute-start(bf16[6,2,48,3072]{3,2,1,0:T(8,128)(2,1)} %pad_maximum_fusion.1), channel_id=1, source_target_pairs={{0,2},{2,4},{4,6},{1,3},{3,5},{5,7},{8,10},{10,12},{12,14},{9,11},... | collective-permute-start | bytes 10616840 | tf_op jit(solution)/shard_map/ppermute | solution.py:18
  165.1 70.6 %collective-permute-start.3 = (bf16[6,2,48,3072]{3,2,1,0:T(8,128)(2,1)}, bf16[6,2,48,3072]{3,2,1,0:T(8,128)(2,1)}, u32[]{:S(2)}, u32[]{:S(2)}) collective-permute-start(bf16[6,2,48,3072]{3,2,1,0:T(8,128)(2,1)} %pad_maximum_fusion.1), channel_id=1, source_target_pairs={{2,0},{4,2},{6,4},{3,1},{5,3},{7,5},{10,8},{12,10},{14,12},{11,9},... | collective-permute-start | bytes 10616840 | tf_op jit(solution)/shard_map/ppermute | solution.py:20
  172.1 63.6 %copy-start.1 = (bf16[2,2,48,3072]{3,2,1,0:T(8,128)(2,1)S(1)}, bf16[2,2,48,3072]{3,2,1,0:T(8,128)(2,1)}, u32[]{:S(2)}) copy-start(bf16[2,2,48,3072]{3,2,1,0:T(8,128)(2,1)} %copy-done) | copy-start | bytes 3538948
  172.1 63.6 %copy-start.3 = (bf16[2,2,48,768]{3,2,1,0:T(8,128)(2,1)S(1)}, bf16[2,2,48,768]{3,2,1,0:T(8,128)(2,1)}, u32[]{:S(2)}) copy-start(bf16[2,2,48,768]{3,2,1,0:T(8,128)(2,1)} %copy-done.2) | copy-start | bytes 884740
  172.1 63.6 %copy-start.5 = (bf16[2,2,48,768]{3,2,1,0:T(8,128)(2,1)S(1)}, bf16[2,2,48,768]{3,2,1,0:T(8,128)(2,1)}, u32[]{:S(2)}) copy-start(bf16[2,2,48,768]{3,2,1,0:T(8,128)(2,1)} %copy-done.4) | copy-start | bytes 884740
  172.2 63.6 %copy-start.7 = (bf16[2,2,48,768]{3,2,1,0:T(8,128)(2,1)S(1)}, bf16[2,2,48,768]{3,2,1,0:T(8,128)(2,1)}, u32[]{:S(2)}) copy-start(bf16[2,2,48,768]{3,2,1,0:T(8,128)(2,1)} %copy-done.6) | copy-start | bytes 884740
  172.2 63.6 %copy-start.9 = (bf16[2,2,48,768]{3,2,1,0:T(8,128)(2,1)S(1)}, bf16[2,2,48,768]{3,2,1,0:T(8,128)(2,1)}, u32[]{:S(2)}) copy-start(bf16[2,2,48,768]{3,2,1,0:T(8,128)(2,1)} %copy-done.8) | copy-start | bytes 884740
  276.3 1.8 copy-start.10
  276.3 1.8 copy-start.11
Sparse Core Ops, SparseCore 0:
  9.7 81.8 all-gather.2
  166.5 38.7 all-gather.4
where the time goes:
time: 454 us; the launch traced here: 450 us
  waiting for transfers between devices  168 us (37%)
  blocking collectives  104 us (23%)
  local copies, waits for them, and re-layouts  71.5 us (16%)
  matrix products  67.9 us (15%)
  between operations  14.3 us (3%)
  other arithmetic  12.9 us (3%)
  starting transfers between devices  11.4 us (3%)
    psum x1, blocking collectives, per_device(): summed = lax.psum(terms, 'mp')  104 us
    all_gather x1, waiting for transfers between devices, per_device(): piece = lax.all_gather(qkv_weight, 'tm', axis=0, tiled=True)  83.6 us
    ppermute x2, waiting for transfers between devices, extended_2(): lax.ppermute(tail, axis, [(i, (i + 1) % count) for i in range(ends)])  63.3 us
    reshape x1, local copies, waits for them, and re-layouts, per_device(): extended.reshape(9 * tile_rows, 4, heads_here, DH)  21.9 us
    ppermute x2, waiting for transfers between devices, extended_2(): lax.ppermute(head, axis, [((i + 1) % count, i) for i in range(ends)])  20.8 us
    all_gather x1, local copies, waits for them, and re-layouts, per_device(): piece = lax.all_gather(qkv_weight, 'tm', axis=0, tiled=True)  18.6 us
    dot_general x6, matrix products, attend(): jnp.dot(query, key_move.T, preferred_element_type=jnp.float32)  10.4 us
    dot_general x1, matrix products, per_device(): jnp.dot(stacked, piece.reshape(piece.shape[0], 3 * local_width), preferre...  10.3 us
  transfers between devices with their start and end apart: 6, of which 5 were waited for; matrix products, arithmetic and copies ran while one was open for 24% of the time, Pallas kernels for 0%

commit v1 on v0

v1 whole, which is shorter than its diff:
```python
import jax
import jax.numpy as jnp
from jax import lax
from jax.experimental import pallas as pl
from jax.experimental.pallas import tpu as pltpu
from jax.sharding import PartitionSpec as P

MESH = pl.DeviceIdType.MESH
T = 192
D = 3072
QT = 48
BF = jnp.bfloat16
F32 = jnp.float32


def kernel(reach, tok, tan, wq, wot, out, tk, w, kv, qb, hs, hid, wz, wo, lsem, ss, rs, ysem, xsem, csem, hsem):
    tm = lax.axis_index("tm")
    y = lax.axis_index("height")
    mp = lax.axis_index("mp")
    x = lax.div(tm, 4)
    zl = lax.rem(lax.div(tm, 2), 2)
    c = lax.rem(tm, 2)
    z = 2 * mp + zl
    oz = 1 - zl
    df = 1 - 2 * c

    def wrap(i):
        return lax.rem(i + 4, 4)

    def dev(xx, yy, zz, cc):
        return (wrap(xx) * 4 + lax.rem(zz, 2) * 2 + cc, wrap(yy), lax.div(zz, 2))

    sib = dev(x, y, z, 1 - c)
    zin = dev(x, y, 2 * mp + oz, c)
    zout = dev(x, y, 2 * (1 - mp) + oz, c)
    zfar = dev(x, y, 2 * (1 - mp) + zl, c)
    xf, xb = dev(x + df, y, z, c), dev(x - df, y, z, c)
    xfar = dev(x + 2, y, z, c)
    xp = dev(x - df, y, z, 1 - c)
    yf, yb = dev(x, y + df, z, c), dev(x, y - df, z, c)
    yup, ydn = dev(x, y + 1, z, c), dev(x, y - 1, z, c)

    peers = (sib, zin, zout, zfar, xf, xb, xfar, xp, yf, yb)
    barrier = pltpu.get_barrier_semaphore()
    for p in peers:
        pl.semaphore_signal(barrier, inc=1, device_id=p, device_id_type=MESH)

    mine = [
        pltpu.make_async_copy(wq.at[zl], w.at[x, zl, c], lsem.at[0]),
        pltpu.make_async_copy(tok, tk.at[0, 0], lsem.at[1]),
        pltpu.make_async_copy(tan, tk.at[0, 1], lsem.at[2]),
        pltpu.make_async_copy(
            wot.at[pl.ds(pl.multiple_of(QT * y, QT), QT)], wz.at[zl, :, pl.ds(pl.multiple_of(mp * 768, 768), 768)], lsem.at[3]
        ),
    ]
    for m in mine:
        m.start()
    pl.semaphore_wait(barrier, len(peers))

    started, from_sib = [], []

    def put(src, dst, where, k):
        cp = pltpu.make_async_remote_copy(
            src_ref=src, dst_ref=dst, send_sem=ss.at[k], recv_sem=rs.at[k], device_id=where, device_id_type=MESH
        )
        cp.start()
        started.append(cp)
        if where is sib:
            from_sib.append(cp)
        return cp

    def rows(yy):
        return pl.ds(pl.multiple_of(QT * wrap(yy), QT), QT)

    yq = rows(y)
    z_w = put(wq.at[oz, yq], w.at[x, zl, c, yq], zin, 0)
    wzl = wz.at[zl, :, pl.ds(pl.multiple_of(mp * 768, 768), 768)]
    z_o = [put(wot.at[yq], wzl, d, 1 + i) for i, d in enumerate((zin, zout, zfar))]
    t0 = put(tok, tk.at[1, 0], zin, 4)
    t1 = put(tan, tk.at[1, 1], zout, 5)
    mine[0].wait()
    z_w.wait_recv()
    q_at = w.at[x, oz, c, yq]
    q_f, q_b = put(q_at, q_at, xf, 6), put(q_at, q_at, xb, 7)
    o_at = w.at[x, zl, c]
    o_f, o_b = put(o_at, o_at, xf, 8), put(o_at, o_at, xb, 9)
    put(o_at, o_at, sib, 10)
    q_f.wait_recv()
    q_at = w.at[wrap(x - df), oz, c, yq]
    q_o = put(q_at, q_at, xf, 11)
    q_b.wait_recv()
    q_o.wait_recv()
    q_at = w.at[:, oz, c, yq]
    y_f, y_b = put(q_at, q_at, yf, 12), put(q_at, q_at, yb, 13)
    put(q_at, q_at, sib, 14)
    o_f.wait_recv()
    o_at = w.at[wrap(x - df), zl, c]
    o_o = put(o_at, o_at, xf, 15)
    put(o_at, o_at, sib, 16)
    y_f.wait_recv()
    q_at = w.at[:, oz, c, rows(y - df)]
    y_o = put(q_at, q_at, yf, 17)
    put(q_at, q_at, sib, 18)
    o_b.wait_recv()
    o_at = w.at[wrap(x + df), zl, c]
    put(o_at, o_at, sib, 19)
    y_b.wait_recv()
    q_at = w.at[:, oz, c, rows(y + df)]
    put(q_at, q_at, sib, 20)
    mine[3].wait()
    for cp in z_o:
        cp.wait_recv()
    holder = lax.div(x, 2) == mp
    mine[1].wait()
    mine[2].wait()
    o_o.wait_recv()
    o_at = w.at[wrap(x + 2), zl, c]
    put(o_at, o_at, sib, 21)
    y_o.wait_recv()
    q_at = w.at[:, oz, c, rows(y + 2)]
    put(q_at, q_at, sib, 22)

    def wo_at(xx, yy):
        return wo.at[lax.rem(xx, 2), :, c, yy]

    def wo_x(d, k):
        return pltpu.make_async_remote_copy(
            src_ref=wz, dst_ref=wo_at(x, y), send_sem=ss.at[k], recv_sem=rs.at[k], device_id=d, device_id_type=MESH
        )

    wo_own = pltpu.make_async_copy(wz, wo_at(x, y), lsem.at[4])
    wo_sends = [wo_x(d, 23 + i) for i, d in enumerate((xf, xb, xfar))]

    @pl.when(holder)
    def _():
        wo_own.start()
        for cp in wo_sends:
            cp.start()

    for cp in from_sib:
        cp.wait_recv()

    def project(i, tau):
        b = 3 * (1 + 2 * tau) + 1

        def lanes(lo, n):
            lhs = tk[i].reshape(2 * T, D)
            return jnp.dot(lhs, w[:, :, :, :, lo : lo + n].reshape(D, n), preferred_element_type=F32).astype(BF)

        for half in range(3):
            r = lanes(384 + 256 * half, 256)
            for part in range(2):
                j = 2 * half + part
                at = (j % 3) * 512 + (j // 3) * 256
                kv[b, :, at : at + 128] = r[:T, part * 128 : part * 128 + 128]
                kv[b, :, at + 128 : at + 256] = r[T:, part * 128 : part * 128 + 128]
        return lanes

    def project_q(i, tau):
        lhs = tk[i].reshape(2 * T, D)
        r = jnp.dot(lhs, w[:, :, :, :, 0:384].reshape(D, 384), preferred_element_type=F32).astype(BF)
        for h in range(3):
            q, qm = r[:T, h * 128 : h * 128 + 128], r[T:, h * 128 : h * 128 + 128]
            qb[tau, h, :T, :128] = q
            qb[tau, h, :T, 128:] = jnp.zeros_like(q)
            qb[tau, h, T:, :128] = qm
            qb[tau, h, T:, 128:] = q

    def head(b, h):
        return kv.at[b, :, pl.ds(pl.multiple_of(h * 512, 512), 512)]

    def far(sems, idx, src, dst, where):
        return pltpu.make_async_remote_copy(
            src_ref=src,
            dst_ref=dst,
            send_sem=sems.at[(0,) + idx],
            recv_sem=sems.at[(1,) + idx],
            device_id=where,
            device_id_type=MESH,
        )

    def y_copy(tau, h, up):
        s = 3 * (1 + 2 * tau)
        return far(ysem, (tau, h, up), head(s + 1, h), head(s + 2 - 2 * up, h), yup if up else ydn)

    def sib_copy(tau, h, dh):
        s = 1 + 2 * tau
        return far(csem, (tau, h, dh), head(3 * s + dh, h), head(3 * (s - df) + dh, h), sib)

    def x_copy(h, dh):
        return far(xsem, (h, dh), head(3 * (1 + 2 * c) + dh, h), head(12 - 12 * c + dh, h), xp)

    def halo(tau):
        for h in range(3):
            y_copy(tau, h, 1).start()
            y_copy(tau, h, 0).start()
        for h in range(3):
            sib_copy(tau, h, 1).start()

    project(0, zl)
    halo(zl)
    project_q(0, zl)
    t0.wait_recv()
    t1.wait_recv()
    project(1, oz)
    halo(oz)
    for h in range(3):
        x_copy(h, 1).start()
    project_q(1, oz)

    for xr in range(2):
        d = lax.rem(2 * mp + xr - x + 4, 4)

        @pl.when(d == 0)
        def _():
            wo_own.wait()

        for i, step in enumerate((4 - df, 4 + df, jnp.int32(2))):

            @pl.when(d == lax.rem(step, 4))
            def _(i=i):
                wo_sends[i].wait_recv()

    quarter = wo.at[:, :, c, y]
    wy_f, wy_b = put(quarter, quarter, yf, 26), put(quarter, quarter, yb, 27)
    put(quarter, quarter, sib, 28)

    def attend(tau, h):
        k = kv[pl.ds(6 * tau, 9), :, pl.ds(pl.multiple_of(h * 512, 256), 256)].reshape(9 * T, 256)
        v = kv[pl.ds(6 * tau, 9), :, pl.ds(pl.multiple_of(h * 512 + 256, 256), 256)].reshape(9 * T, 256)
        both = lax.dot_general(qb[tau, h], k, (((1,), (1,)), ((), ())), preferred_element_type=F32)
        tile = 4 * x + 2 * tau + c
        hid_h = 3 * zl + h
        low = jnp.float32(-1e30)
        zero = jnp.float32(0.0)
        rf, rr = reach[0, hid_h], reach[1, hid_h]
        left = jnp.where((rf >= 1) & (tile > 0), zero, low)
        right = jnp.where((rf >= 1) & (tile < 15), zero, low)
        above = jnp.where((rr >= 1) & (y > 0), zero, low)
        below = jnp.where((rr >= 1) & (y < 3), zero, low)
        col = lax.broadcasted_iota(jnp.int32, (1, 9 * T), 1)
        bias = jnp.where(col < 3 * T, left, jnp.where(col >= 6 * T, right, zero))
        row = col - jnp.where(col < 3 * T, 0, jnp.where(col >= 6 * T, 6 * T, 3 * T))
        bias = bias + jnp.where(row < T, above, jnp.where(row >= 2 * T, below, zero))
        factor = 1.0 / 128**0.5
        s = both[:T] * factor + bias
        e = jnp.exp(s - jnp.max(s, axis=-1, keepdims=True))
        p = e * (1.0 / jnp.sum(e, axis=-1, keepdims=True))
        m = p * (both[T:] * factor)
        shift = jnp.sum(m, axis=-1, keepdims=True)
        lhs = jnp.concatenate([p.astype(BF), m.astype(BF)], 0)
        r = jnp.dot(lhs, v, preferred_element_type=F32)
        o = r[:T, :128]
        om = r[:T, 128:] + r[T:, :128] - o * shift
        at = pl.ds(pl.multiple_of(h * 128, 128), 128)
        hs[tau, :T, at] = o.astype(BF)
        hs[tau, T:, at] = om.astype(BF)

    def hid_copies(tau, h):
        at = pl.ds(pl.multiple_of(h * 128, 128), 128)
        src = hs.at[tau, :, at]
        dst = hid.at[:, pl.ds(pl.multiple_of(z * 384 + h * 128, 128), 128)]
        own = pltpu.make_async_copy(src, dst, lsem.at[5 + h])
        return own, [far(hsem, (i, h), src, dst, d) for i, d in enumerate((zin, zout, zfar))]

    def send_hidden(tau, h):
        own, (a, b, f) = hid_copies(tau, h)

        @pl.when(tau == zl)
        def _():
            own.start()
            f.start()

        @pl.when(tau != zl)
        def _():
            a.start()
            b.start()

    def first(h, carry):
        for up in range(2):
            y_copy(c, h, up).wait_recv()
        for dh in (0, 2):
            x_copy(h, dh).start()
            sib_copy(c, h, dh).start()
        for up in range(2):
            y_copy(1 - c, h, up).wait_recv()
        for dh in (0, 2):
            sib_copy(1 - c, h, dh).start()
        for tau in range(2):
            for dh in range(3):
                sib_copy(tau, h, dh).wait_recv()
        attend(1 - c, h)
        send_hidden(1 - c, h)
        return carry

    lax.fori_loop(0, 3, first, 0)

    wy_f.wait_recv()
    quarter = wo.at[:, :, c, wrap(y - df)]
    wy_o = put(quarter, quarter, yf, 29)
    put(quarter, quarter, sib, 30)

    def second(h, carry):
        for dh in range(3):
            x_copy(h, dh).wait_recv()
        attend(c, h)
        send_hidden(c, h)
        return carry

    lax.fori_loop(0, 3, second, 0)

    wy_b.wait_recv()
    quarter = wo.at[:, :, c, wrap(y + df)]
    put(quarter, quarter, sib, 31)
    wy_o.wait_recv()
    quarter = wo.at[:, :, c, wrap(y + 2)]
    put(quarter, quarter, sib, 32)
    for cp in from_sib[8:]:
        cp.wait_recv()

    for h in range(3):
        own, remote = hid_copies(zl, h)
        own.wait()
        for cp in remote:
            cp.wait_recv()

    for a in range(2):
        r = lax.dot_general(
            hid[...], wo[a].reshape(768, 1536), (((1,), (1,)), ((), ())), preferred_element_type=F32
        )
        out[:, a * 768 : a * 768 + 768] = r.astype(BF)

    for cp in started:
        cp.wait_send()

    @pl.when(holder)
    def _():
        for cp in wo_sends:
            cp.wait_send()

    def drain(h, carry):
        for tau in range(2):
            for up in range(2):
                y_copy(tau, h, up).wait_send()
            for dh in range(3):
                sib_copy(tau, h, dh).wait_send()
        for dh in range(3):
            x_copy(h, dh).wait_send()
        own, remote = hid_copies(zl, h)
        for cp in remote:
            cp.wait_send()
        return carry

    lax.fori_loop(0, 3, drain, 0)


def per_device(tokens, tangent, qkv_weight, out_weight, reach):
    any_spec = pl.BlockSpec(memory_space=pl.ANY)
    wq = jnp.transpose(qkv_weight.reshape(T, 3, 2, 384), (2, 0, 1, 3)).reshape(2, T, 1152)
    dma = pltpu.SemaphoreType.DMA
    out = pl.pallas_call(
        kernel,
        out_shape=jax.ShapeDtypeStruct((2 * T, 1536), BF),
        in_specs=[pl.BlockSpec(memory_space=pltpu.SMEM)] + [any_spec] * 4,
        out_specs=pl.BlockSpec(memory_space=pltpu.VMEM),
        scratch_shapes=[
            pltpu.VMEM((2, 2, T, D), BF),
            pltpu.VMEM((4, 2, 2, T, 1152), BF),
            pltpu.VMEM((15, T, 1536), BF),
            pltpu.VMEM((2, 3, 2 * T, 256), BF),
            pltpu.VMEM((2, 2 * T, 384), BF),
            pltpu.VMEM((2 * T, 1536), BF),
            pltpu.VMEM((2, QT, 1536), BF),
            pltpu.VMEM((2, 2, 2, 4, QT, 1536), BF),
            dma((8,)),
            dma((33,)),
            dma((33,)),
            dma((2, 2, 3, 2)),
            dma((2, 3, 3)),
            dma((2, 2, 3, 3)),
            dma((2, 3, 3)),
        ],
        compiler_params=pltpu.CompilerParams(
            collective_id=0, has_side_effects=True, vmem_limit_bytes=60 * 1024 * 1024
        ),
    )(reach, tokens.reshape(T, D), tangent.reshape(T, D), wq, out_weight.T)
    both = out.reshape(2, 2, 2, 48, 1536)
    return both[0], both[1]


def solution(mesh):
    in_specs = (
        P("tm", "height", None, None),
        P("tm", "height", None, None),
        P("tm", None, "mp"),
        P("mp", "tm"),
        P(None, "mp"),
    )
    out_specs = (P("tm", "height", None, "mp"), P("tm", "height", None, "mp"))
    return jax.shard_map(per_device, mesh=mesh, in_specs=in_specs, out_specs=out_specs, check_vma=False)
```

time: 454 us -> 109 us (0.24)
  the two profiles are of different devices: /device:TPU:7 before, /device:TPU:1 now
where the time goes in v1:
time: 109 us; the launch traced here: 108 us
  Pallas kernels  99.8 us (92%)
  local copies, waits for them, and re-layouts  7.24 us (7%)
    pallas_call x1, Pallas kernels, per_device(): pl.pallas_call(kernel, out_shape=jax.ShapeDtypeStruct((2 * T, 1536), BF),...  99.8 us
    reshape x2, local copies, waits for them, and re-layouts, per_device(): qkv_weight.reshape(T, 3, 2, 384)  2.94 us
    slice x1, local copies, waits for them, and re-layouts, per_device(): return (both[0], both[1])  2.33 us

profile of v1, /device:TPU:1, one launch (start us, length us, event | category | flops | bytes accessed | tf_op | source)
XLA Modules:
  0.0 107.6 jit_solution(12741461043577978650)
XLA Ops:
  0.6 2.2 %reshape.23 = bf16[192,3,2,384]{3,2,0,1:T(2,128)(2,1)S(1)} reshape(bf16[192,3,768]{2,0,1:T(8,128)(2,1)} %param.7) | data formatting | bytes 1769472 | tf_op jit(solution)/shard_map/reshape | solution.py:359
  2.8 0.8 copy.10
  3.6 2.0 %reshape.24.wq = bf16[2,192,1152]{2,1,0:T(8,128)(2,1)} reshape(bf16[2,192,3,384]{3,2,1,0:T(4,128)(2,1)S(1)} %bitcast.10) | data formatting | bytes 1769472 | tf_op jit(solution)/shard_map/reshape | solution.py:359
  5.6 99.8 %shard_map.68 = bf16[384,1536]{1,0:T(8,128)(2,1)} custom-call(s32[2,6]{1,0:T(2,128)} %reach.1, bf16[192,3072]{1,0:T(8,128)(2,1)} %bitcast.11, bf16[192,3072]{1,0:T(8,128)(2,1)} %bitcast.12, bf16[2,192,1152]{2,1,0:T(8,128)(2,1)} %reshape.24.wq, bf16[192,768]{1,0:T(8,128)(2,1)} %bitcast.15), custom_call_target="tpu_custom_call" | custom-call | tf_op jit(solution)/shard_map/pallas_call | solution.py:361
  105.3 2.3 %fusion = (bf16[192,1536]{1,0:T(8,128)(2,1)}, bf16[192,1536]{1,0:T(8,128)(2,1)}) fusion(bf16[384,1536]{1,0:T(8,128)(2,1)} %shard_map.68), kind=kLoop, calls=%fused_computation.1 | loop fusion | bytes 2359296 | tf_op jit(solution)/shard_map/slice | solution.py:388

commit v2 on v1

v2 whole, which is shorter than its diff:
```python
import jax
import jax.numpy as jnp
from jax import lax
from jax.experimental import pallas as pl
from jax.experimental.pallas import tpu as pltpu
from jax.sharding import PartitionSpec as P

MESH = pl.DeviceIdType.MESH
T = 192
D = 3072
QT = 48
BF = jnp.bfloat16
SENDS = 80
F32 = jnp.float32


def kernel(reach, tok, tan, wq, wot, out0, out1, tk, wk, wqb, kv, qb, hs, hid, wz, wo, lsem, ss, rs, osem, ysem, xsem, csem, hsem):
    tm = lax.axis_index("tm")
    y = lax.axis_index("height")
    mp = lax.axis_index("mp")
    x = lax.div(tm, 4)
    zl = lax.rem(lax.div(tm, 2), 2)
    c = lax.rem(tm, 2)
    z = 2 * mp + zl
    oz = 1 - zl
    df = 1 - 2 * c
    pe = 1 - 2 * lax.rem(x, 2)

    def wrap(i):
        return lax.rem(i + 4, 4)

    def dev(xx, yy, zz, cc):
        return (wrap(xx) * 4 + lax.rem(zz, 2) * 2 + cc, wrap(yy), lax.div(zz, 2))

    sib = dev(x, y, z, 1 - c)
    zin = dev(x, y, 2 * mp + oz, c)
    zout = dev(x, y, 2 * (1 - mp) + oz, c)
    zfar = dev(x, y, 2 * (1 - mp) + zl, c)
    xf, xb, xfar = dev(x + df, y, z, c), dev(x - df, y, z, c), dev(x + 2, y, z, c)
    xpair, xnext = dev(x + pe, y, z, c), dev(x - pe, y, z, c)
    xp = dev(x - df, y, z, 1 - c)
    yf, yb = dev(x, y + df, z, c), dev(x, y - df, z, c)
    yup, ydn = dev(x, y + 1, z, c), dev(x, y - 1, z, c)

    peers = (sib, zin, zout, zfar, xf, xb, xfar, xp, yf, yb)
    barrier = pltpu.get_barrier_semaphore()
    for p in peers:
        pl.semaphore_signal(barrier, inc=1, device_id=p, device_id_type=MESH)

    def rows(yy):
        return pl.ds(pl.multiple_of(QT * wrap(yy), QT), QT)

    yq = rows(y)
    ALL = slice(None)
    holder = lax.div(x, 2) == mp
    me2 = lax.rem(x, 2)

    def chunk_src(n, g, r):
        if n == 3:
            return wq.at[0, r, pl.ds(pl.multiple_of(g * 384, 384), 384)]
        return wq.at[pl.ds(1, 2), r, pl.ds(pl.multiple_of(g * 384 + n * 128, 128), 128)]

    def chunk(n, xx, zz, r):
        return wqb.at[xx, zz, c, r] if n == 3 else wk.at[n, :, xx, zz, c, r]

    def wz_at(q):
        return wz.at[q, zl, :, pl.ds(pl.multiple_of(mp * 768, 768), 768)]

    mine = [pltpu.make_async_copy(chunk_src(n, zl, ALL), chunk(n, x, zl, ALL), lsem.at[n]) for n in range(4)]
    mine += [
        pltpu.make_async_copy(tok, tk.at[0, 0], lsem.at[4]),
        pltpu.make_async_copy(tan, tk.at[0, 1], lsem.at[5]),
        pltpu.make_async_copy(wot.at[yq], wz_at(0), lsem.at[6]),
        pltpu.make_async_copy(wot.at[rows(y + 2)], wz_at(1), lsem.at[7]),
    ]
    for m in mine:
        m.start()
    pl.semaphore_wait(barrier, len(peers))

    started = []

    def put(src, dst, where):
        k = len(started)
        cp = pltpu.make_async_remote_copy(
            src_ref=src, dst_ref=dst, send_sem=ss.at[k], recv_sem=rs.at[k], device_id=where, device_id_type=MESH
        )
        cp.start()
        started.append(cp)
        return cp

    def same(ref, where):
        return put(ref, ref, where)

    def arrived(*copies):
        for cp in copies:
            cp.wait_recv()

    def o_copy(src, dst, where, k):
        return pltpu.make_async_remote_copy(
            src_ref=src, dst_ref=dst, send_sem=osem.at[0, k], recv_sem=osem.at[1, k], device_id=where, device_id_type=MESH
        )

    def wo_z(q, i):
        return o_copy(wot.at[rows(y + 2 * q)], wz_at(q), (zin, zout, zfar)[i], 3 * q + i)

    xl, xr, xo = wrap(x - df), wrap(x + df), wrap(x + 2)
    z_w, o_f, o_b, o_o, x_q, y_f, y_b, y_o = ({} for _ in range(8))
    sibs = [[] for _ in range(4)]

    def own_rows(n):
        src, dst = chunk_src(n, zl, ALL), chunk(n, x, zl, ALL)
        o_f[n], o_b[n] = put(src, dst, xf), put(src, dst, xb)
        sibs[n].append(put(src, dst, sib))

    def share(n, ref):
        sibs[n].append(same(ref, sib))

    def quarter_x(n):
        arrived(z_w[n])
        x_q[n] = [same(chunk(n, x, oz, yq), d) for d in (xf, xb, xfar)]

    def own_relay(n):
        arrived(o_f[n])
        o_o[n] = same(chunk(n, xl, zl, ALL), xf)
        share(n, chunk(n, xl, zl, ALL))

    def quarter_y(n):
        arrived(*x_q[n])
        ref = chunk(n, ALL, oz, yq)
        y_f[n], y_b[n] = same(ref, yf), same(ref, yb)
        share(n, ref)

    def relay_y(n):
        arrived(o_b[n])
        share(n, chunk(n, xr, zl, ALL))
        arrived(y_f[n])
        ref = chunk(n, ALL, oz, rows(y - df))
        y_o[n] = same(ref, yf)
        share(n, ref)

    def last_y(n):
        arrived(y_b[n])
        share(n, chunk(n, ALL, oz, rows(y + df)))
        arrived(o_o[n])
        share(n, chunk(n, xo, zl, ALL))
        arrived(y_o[n])
        share(n, chunk(n, ALL, oz, rows(y + 2)))

    def project(i, tau, h):
        b = 3 * (1 + 2 * tau) + 1
        lhs = tk[i].reshape(2 * T, D)
        rhs = jnp.concatenate([wk[h, j].reshape(D, 128) for j in range(2)], 1)
        r = jnp.dot(lhs, rhs, preferred_element_type=F32).astype(BF)
        for j in range(2):
            at = h * 512 + j * 256
            kv[b, :, at : at + 128] = r[:T, j * 128 : j * 128 + 128]
            kv[b, :, at + 128 : at + 256] = r[T:, j * 128 : j * 128 + 128]

    def project_q(i, tau):
        lhs = tk[i].reshape(2 * T, D)
        r = jnp.dot(lhs, wqb[...].reshape(D, 384), preferred_element_type=F32).astype(BF)
        for h in range(3):
            q, qm = r[:T, h * 128 : h * 128 + 128], r[T:, h * 128 : h * 128 + 128]
            qb[tau, h, :T, :128] = q
            qb[tau, h, :T, 128:] = jnp.zeros_like(q)
            qb[tau, h, T:, :128] = qm
            qb[tau, h, T:, 128:] = q

    def head(b, h):
        return kv.at[b, :, pl.ds(pl.multiple_of(h * 512, 512), 512)]

    def far(sems, idx, src, dst, where):
        return pltpu.make_async_remote_copy(
            src_ref=src,
            dst_ref=dst,
            send_sem=sems.at[(0,) + idx],
            recv_sem=sems.at[(1,) + idx],
            device_id=where,
            device_id_type=MESH,
        )

    def y_copy(tau, h, up):
        s = 3 * (1 + 2 * tau)
        return far(ysem, (tau, h, up), head(s + 1, h), head(s + 2 - 2 * up, h), yup if up else ydn)

    def sib_copy(tau, h, dh):
        s = 1 + 2 * tau
        return far(csem, (tau, h, dh), head(3 * s + dh, h), head(3 * (s - df) + dh, h), sib)

    def x_copy(h, dh):
        return far(xsem, (h, dh), head(3 * (1 + 2 * c) + dh, h), head(12 - 12 * c + dh, h), xp)

    def halo(tau, h, edge):
        y_copy(tau, h, 1).start()
        y_copy(tau, h, 0).start()
        sib_copy(tau, h, 1).start()

        @pl.when(edge)
        def _():
            x_copy(h, 1).start()

    def wo_at(slot, q, zz):
        return wo.at[slot, zz, c, wrap(y + 2 * q)]

    def wo_pair(src, slot, q, zz):
        return o_copy(src, wo_at(slot, q, zz), xpair, 6 + 2 * q + zz)

    def wo_next(q, zz):
        return o_copy(wz.at[q, zz], wo_at(me2, q, zz), xnext, 10 + 2 * q + zz)

    def wo_own(q, zz):
        return pltpu.make_async_copy(wz.at[q, zz], wo_at(me2, q, zz), lsem.at[11 + 2 * q + zz])

    def wo_relay(q, zz):
        @pl.when(jnp.logical_not(holder))
        def _():
            wo_next(q, zz).wait_recv()
            wo_pair(wo_at(1 - me2, q, zz), 1 - me2, q, zz).start()

    def own_tile(h):
        last_y(h)
        arrived(*sibs[h])
        project(0, zl, h)
        halo(zl, h, zl == c)

    for n in range(4):
        z_w[n] = put(chunk_src(n, oz, yq), chunk(n, x, zl, yq), zin)
    own_rows(0)
    for q in range(2):

        @pl.when(holder)
        def _(q=q):
            wo_z(q, 0).start()

        @pl.when(jnp.logical_not(holder))
        def _(q=q):
            wo_z(q, 1).start()
            wo_z(q, 2).start()

    t0 = put(tok, tk.at[1, 0], zin)
    t1 = put(tan, tk.at[1, 1], zout)
    for n in range(4):
        quarter_x(n)
    def own_halo(h, carry):
        for up in range(2):
            y_copy(zl, h, up).wait_recv()
        for dh in (0, 2):
            sib_copy(zl, h, dh).start()

        @pl.when(zl == c)
        def _():
            for dh in (0, 2):
                x_copy(h, dh).start()

        return carry

    def partner_start(h):
        halo(oz, h, zl != c)

    def wo_first(q):
        @pl.when(holder)
        def _():
            for i in range(3):
                wo_z(q, i).wait_recv()
            for zz in range(2):
                wo_next(q, zz).start()
                wo_pair(wz.at[q, zz], me2, q, zz).start()
                wo_own(q, zz).start()

    own_relay(0)
    own_rows(1)
    own_rows(2)
    for n in range(3):
        quarter_y(n)
    relay_y(0)
    own_relay(1)
    relay_y(1)
    for m in mine:
        m.wait()
    wo_first(0)
    own_tile(0)
    own_relay(2)
    own_rows(3)
    wo_first(1)
    relay_y(2)
    own_tile(1)
    own_tile(2)
    wo_relay(0, 0)
    own_relay(3)
    quarter_y(3)
    wo_relay(0, 1)
    own_halo(0, 0)
    relay_y(3)
    arrived(t0, t1)
    for h in range(3):
        project(1, oz, h)

        @pl.when(zl != c)
        def _(h=h):
            partner_start(h)

    wo_relay(1, 0)
    lax.fori_loop(1, 3, own_halo, 0)

    @pl.when(zl == c)
    def _():
        for h in range(3):
            partner_start(h)

    wo_relay(1, 1)
    last_y(3)
    arrived(*sibs[3])
    project_q(0, zl)
    project_q(1, oz)

    def attend(tau, h):
        k = kv[pl.ds(6 * tau, 9), :, pl.ds(pl.multiple_of(h * 512, 256), 256)].reshape(9 * T, 256)
        v = kv[pl.ds(6 * tau, 9), :, pl.ds(pl.multiple_of(h * 512 + 256, 256), 256)].reshape(9 * T, 256)
        both = lax.dot_general(qb[tau, h], k, (((1,), (1,)), ((), ())), preferred_element_type=F32)
        tile = 4 * x + 2 * tau + c
        hid_h = 3 * zl + h
        low = jnp.float32(-1e30)
        zero = jnp.float32(0.0)
        rf, rr = reach[0, hid_h], reach[1, hid_h]
        left = jnp.where((rf >= 1) & (tile > 0), zero, low)
        right = jnp.where((rf >= 1) & (tile < 15), zero, low)
        above = jnp.where((rr >= 1) & (y > 0), zero, low)
        below = jnp.where((rr >= 1) & (y < 3), zero, low)
        col = lax.broadcasted_iota(jnp.int32, (1, 9 * T), 1)
        bias = jnp.where(col < 3 * T, left, jnp.where(col >= 6 * T, right, zero))
        row = col - jnp.where(col < 3 * T, 0, jnp.where(col >= 6 * T, 6 * T, 3 * T))
        bias = bias + jnp.where(row < T, above, jnp.where(row >= 2 * T, below, zero))
        factor = 1.0 / 128**0.5
        s = both[:T] * factor + bias
        e = jnp.exp(s - jnp.max(s, axis=-1, keepdims=True))
        p = e * (1.0 / jnp.sum(e, axis=-1, keepdims=True))
        m = p * (both[T:] * factor)
        shift = jnp.sum(m, axis=-1, keepdims=True)
        lhs = jnp.concatenate([p.astype(BF), m.astype(BF)], 0)
        r = jnp.dot(lhs, v, preferred_element_type=F32)
        o = r[:T, :128]
        om = r[:T, 128:] + r[T:, :128] - o * shift
        at = pl.ds(pl.multiple_of(h * 128, 128), 128)
        hs[tau, :T, at] = o.astype(BF)
        hs[tau, T:, at] = om.astype(BF)

    def hid_copies(tau, h):
        at = pl.ds(pl.multiple_of(h * 128, 128), 128)
        src = hs.at[tau, :, at]
        dst = hid.at[:, pl.ds(pl.multiple_of(z * 384 + h * 128, 128), 128)]
        own = pltpu.make_async_copy(src, dst, lsem.at[8 + h])
        return own, [far(hsem, (i, h), src, dst, d) for i, d in enumerate((zin, zout, zfar))]

    def send_hidden(tau, h):
        own, (a, b, f) = hid_copies(tau, h)

        @pl.when(tau == zl)
        def _():
            own.start()
            f.start()

        @pl.when(tau != zl)
        def _():
            a.start()
            b.start()

    def partner_halo(h):
        for up in range(2):
            y_copy(oz, h, up).wait_recv()

        @pl.when(zl != c)
        def _():
            for dh in (0, 2):
                x_copy(h, dh).start()

        for dh in (0, 2):
            sib_copy(oz, h, dh).start()

    def inner(h):
        for tau in range(2):
            for dh in range(3):
                sib_copy(tau, h, dh).wait_recv()
        attend(1 - c, h)
        send_hidden(1 - c, h)

    def edge(h):
        for dh in range(3):
            x_copy(h, dh).wait_recv()
        attend(c, h)
        send_hidden(c, h)

    def wo_ready(q):
        for zz in range(2):
            wo_pair(wz.at[q, zz], me2, q, zz).wait_recv()

            @pl.when(holder)
            def _(zz=zz):
                wo_own(q, zz).wait()

    partner_halo(0)
    inner(0)
    wo_ready(0)

    def middle(h, carry):
        partner_halo(h)

        @pl.when(h == 2)
        def _():
            for cp in wy:
                cp.start()

        inner(h)
        edge(h - 1)
        return carry

    quarter = wo.at[:, :, c, y]
    wy = [o_copy(quarter, quarter, d, 14 + i) for i, d in enumerate((yf, yb))]
    lax.fori_loop(1, 3, middle, 0)
    o_sib = [same(quarter, sib)]
    edge(2)

    wo_ready(1)
    o_sib.append(same(wo.at[:, :, c, wrap(y + 2)], sib))
    for i, cp in enumerate(wy):
        arrived(cp)
        o_sib.append(same(wo.at[:, :, c, wrap(y - df + 2 * df * i)], sib))
    arrived(*o_sib)

    for h in range(3):
        own, remote = hid_copies(zl, h)
        own.wait()
        for cp in remote:
            cp.wait_recv()

    for a in range(2):
        r = lax.dot_general(
            hid[...], wo[a].reshape(768, 1536), (((1,), (1,)), ((), ())), preferred_element_type=F32
        ).astype(BF)
        for f in range(2):
            for i in range(2):
                at = (2 * f + i) * 48
                out0[f, i, :, a * 768 : a * 768 + 768] = r[at : at + 48]
                out1[f, i, :, a * 768 : a * 768 + 768] = r[T + at : T + at + 48]

    for cp in started + wy:
        cp.wait_send()

    for q in range(2):
        for zz in range(2):
            wo_pair(wz.at[q, zz], me2, q, zz).wait_send()

            @pl.when(holder)
            def _(q=q, zz=zz):
                wo_next(q, zz).wait_send()

        @pl.when(holder)
        def _(q=q):
            wo_z(q, 0).wait_send()

        @pl.when(jnp.logical_not(holder))
        def _(q=q):
            wo_z(q, 1).wait_send()
            wo_z(q, 2).wait_send()

    def drain(h, carry):
        for tau in range(2):
            for up in range(2):
                y_copy(tau, h, up).wait_send()
            for dh in range(3):
                sib_copy(tau, h, dh).wait_send()
        for dh in range(3):
            x_copy(h, dh).wait_send()
        own, remote = hid_copies(zl, h)
        for cp in remote:
            cp.wait_send()
        return carry

    lax.fori_loop(0, 3, drain, 0)


def per_device(tokens, tangent, qkv_weight, out_weight, reach):
    any_spec = pl.BlockSpec(memory_space=pl.ANY)
    vmem = pl.BlockSpec(memory_space=pltpu.VMEM)
    dma = pltpu.SemaphoreType.DMA
    result = jax.ShapeDtypeStruct((2, 2, 48, 1536), BF)
    return pl.pallas_call(
        kernel,
        out_shape=(result, result),
        in_specs=[pl.BlockSpec(memory_space=pltpu.SMEM)] + [any_spec] * 4,
        out_specs=(vmem, vmem),
        scratch_shapes=[
            pltpu.VMEM((2, 2, T, D), BF),
            pltpu.VMEM((3, 2, 4, 2, 2, T, 128), BF),
            pltpu.VMEM((4, 2, 2, T, 384), BF),
            pltpu.VMEM((15, T, 1536), BF),
            pltpu.VMEM((2, 3, 2 * T, 256), BF),
            pltpu.VMEM((2, 2 * T, 384), BF),
            pltpu.VMEM((2 * T, 1536), BF),
            pltpu.VMEM((2, 2, QT, 1536), BF),
            pltpu.VMEM((2, 2, 2, 4, QT, 1536), BF),
            dma((15,)),
            dma((SENDS,)),
            dma((SENDS,)),
            dma((2, 16)),
            dma((2, 2, 3, 2)),
            dma((2, 3, 3)),
            dma((2, 2, 3, 3)),
            dma((2, 3, 3)),
        ],
        compiler_params=pltpu.CompilerParams(
            collective_id=0, has_side_effects=True, vmem_limit_bytes=60 * 1024 * 1024
        ),
    )(reach, tokens.reshape(T, D), tangent.reshape(T, D), jnp.transpose(qkv_weight, (1, 0, 2)), out_weight.T)


def solution(mesh):
    in_specs = (
        P("tm", "height", None, None),
        P("tm", "height", None, None),
        P("tm", None, "mp"),
        P("mp", "tm"),
        P(None, "mp"),
    )
    out_specs = (P("tm", "height", None, "mp"), P("tm", "height", None, "mp"))
    return jax.shard_map(per_device, mesh=mesh, in_specs=in_specs, out_specs=out_specs, check_vma=False)
```

time: 109 us -> 93.5 us (0.86); the launches traced: 108 us -> 93.4 us
  Pallas kernels: 99.8 us -> 89.9 us
  local copies, waits for them, and re-layouts: 7.24 us -> 2.8 us
    pallas_call x1, Pallas kernels: 99.8 us -> 89.9 us  [per_device(): pl.pallas_call(kernel, out_shape=(result, result), in_specs=[pl.BlockSpec...]
    reshape x3 -> x0, local copies, waits for them, and re-layouts: 4.91 us -> none  [the longest x2 2.94 us: per_device(): qkv_weight.reshape(T, 3, 2, 384)]
    unnamed x0 -> x4, local copies, waits for them, and re-layouts: none -> 2.8 us
    slice x1 -> x0, local copies, waits for them, and re-layouts: 2.33 us -> none  [per_device(): return (both[0], both[1])]
where the time goes in v2:
time: 93.5 us; the launch traced here: 93.4 us
  Pallas kernels  89.9 us (96%)
  local copies, waits for them, and re-layouts  2.8 us (3%)
    pallas_call x1, Pallas kernels, per_device(): pl.pallas_call(kernel, out_shape=(result, result), in_specs=[pl.BlockSpec...  89.9 us
    unnamed x4, local copies, waits for them, and re-layouts  2.8 us

profile of v2, /device:TPU:1, one launch (start us, length us, event | category | flops | bytes accessed | tf_op | source)
XLA Modules:
  0.0 93.4 jit_solution(15011930003711808327)
XLA Ops:
  0.6 89.9 %shard_map.68 = (bf16[2,2,48,1536]{3,2,1,0:T(8,128)(2,1)}, bf16[2,2,48,1536]{3,2,1,0:T(8,128)(2,1)}) custom-call(s32[2,6]{1,0:T(2,128)} %reach.1, bf16[192,3072]{1,0:T(8,128)(2,1)} %bitcast.4, bf16[192,3072]{1,0:T(8,128)(2,1)} %bitcast.5, bf16[3,192,768]{2,1,0:T(8,128)(2,1)} %bitcast.6, bf16[192,768]{1,0:T(8,128)(2,1)} %bitcast.7), custom_call_target="tpu_custom_call" | custom-call | tf_op jit(solution)/shard_map/pallas_call | solution.py:486
  90.6 0.0 copy-start
  90.6 2.0 %copy.9 = bf16[2,2,48,1536]{3,2,1,0:T(8,128)(2,1)} copy(bf16[2,2,48,1536]{3,2,1,0:T(8,128)(2,1)} %get-tuple-element.4) | data formatting | bytes 1179648
  92.5 0.0 copy-done
  92.6 0.8 copy.10
Async XLA Ops:
  90.6 2.0 %copy-start = (bf16[2,2,48,1536]{3,2,1,0:T(8,128)(2,1)S(1)}, bf16[2,2,48,1536]{3,2,1,0:T(8,128)(2,1)}, u32[]{:S(2)}) copy-start(bf16[2,2,48,1536]{3,2,1,0:T(8,128)(2,1)} %get-tuple-element.5) | copy-start | bytes 1769476

commit v3 on v2

--- a/solution.py
+++ b/solution.py
@@ -10,7 +10,7 @@
 D = 3072
 QT = 48
 BF = jnp.bfloat16
-SENDS = 80
+SENDS = 104
 F32 = jnp.float32
 
 
@@ -117,7 +117,9 @@
 
     def quarter_x(n):
         arrived(z_w[n])
-        x_q[n] = [same(chunk(n, x, oz, yq), d) for d in (xf, xb, xfar)]
+        ref = chunk(n, x, oz, yq)
+        x_q[n] = [same(ref, d) for d in (xf, xb, xfar)]
+        y_f[n], y_b[n] = [same(ref, yf)], [same(ref, yb)]
 
     def own_relay(n):
         arrived(o_f[n])
@@ -125,21 +127,23 @@
         share(n, chunk(n, xl, zl, ALL))
 
     def quarter_y(n):
-        arrived(*x_q[n])
-        ref = chunk(n, ALL, oz, yq)
-        y_f[n], y_b[n] = same(ref, yf), same(ref, yb)
-        share(n, ref)
+        for cp, xx in zip(x_q[n], (xl, xr, xo)):
+            arrived(cp)
+            ref = chunk(n, xx, oz, yq)
+            y_f[n].append(same(ref, yf))
+            y_b[n].append(same(ref, yb))
+        share(n, chunk(n, ALL, oz, yq))
 
     def relay_y(n):
         arrived(o_b[n])
         share(n, chunk(n, xr, zl, ALL))
-        arrived(y_f[n])
+        arrived(*y_f[n])
         ref = chunk(n, ALL, oz, rows(y - df))
         y_o[n] = same(ref, yf)
         share(n, ref)
 
     def last_y(n):
-        arrived(y_b[n])
+        arrived(*y_b[n])
         share(n, chunk(n, ALL, oz, rows(y + df)))
         arrived(o_o[n])
         share(n, chunk(n, xo, zl, ALL))
@@ -218,7 +222,6 @@
             wo_pair(wo_at(1 - me2, q, zz), 1 - me2, q, zz).start()
 
     def own_tile(h):
-        last_y(h)
         arrived(*sibs[h])
         project(0, zl, h)
         halo(zl, h, zl == c)
@@ -275,37 +278,33 @@
     relay_y(0)
     own_relay(1)
     relay_y(1)
+    last_y(0)
+    quarter_y(3)
+    own_relay(2)
+    own_rows(3)
+    relay_y(2)
     for m in mine:
         m.wait()
     wo_first(0)
     own_tile(0)
-    own_relay(2)
-    own_rows(3)
+    last_y(1)
+    own_tile(1)
+    last_y(2)
+    relay_y(3)
     wo_first(1)
-    relay_y(2)
-    own_tile(1)
     own_tile(2)
     wo_relay(0, 0)
     own_relay(3)
-    quarter_y(3)
     wo_relay(0, 1)
     own_halo(0, 0)
-    relay_y(3)
     arrived(t0, t1)
     for h in range(3):
         project(1, oz, h)
 
-        @pl.when(zl != c)
-        def _(h=h):
-            partner_start(h)
+        partner_start(h)
 
     wo_relay(1, 0)
     lax.fori_loop(1, 3, own_halo, 0)
-
-    @pl.when(zl == c)
-    def _():
-        for h in range(3):
-            partner_start(h)
 
     wo_relay(1, 1)
     last_y(3)
@@ -397,27 +396,55 @@
             def _(zz=zz):
                 wo_own(q, zz).wait()
 
+    wo_ready(0)
+
+    quarter = wo.at[:, :, c, y]
+    wy = [o_copy(quarter, quarter, d, 14 + i) for i, d in enumerate((yf, yb))]
     partner_halo(0)
     inner(0)
-    wo_ready(0)
-
-    def middle(h, carry):
-        partner_halo(h)
-
-        @pl.when(h == 2)
-        def _():
-            for cp in wy:
-                cp.start()
-
-        inner(h)
-        edge(h - 1)
-        return carry
-
-    quarter = wo.at[:, :, c, y]
-    wy = [o_copy(quarter, quarter, d, 14 + i) for i, d in enumerate((yf, yb))]
-    lax.fori_loop(1, 3, middle, 0)
+    partner_halo(1)
+    inner(1)
+    partner_halo(2)
+    for cp in wy:
+        cp.start()
+    edge(0)
+    inner(2)
+    edge(1)
     o_sib = [same(quarter, sib)]
     edge(2)
+
+    for cp in started:
+        cp.wait_send()
+    drained = len(started)
+
+    for q in range(2):
+        for zz in range(2):
+            wo_pair(wz.at[q, zz], me2, q, zz).wait_send()
+
+            @pl.when(holder)
+            def _(q=q, zz=zz):
+                wo_next(q, zz).wait_send()
+
+        @pl.when(holder)
+        def _(q=q):
+            wo_z(q, 0).wait_send()
+
+        @pl.when(jnp.logical_not(holder))
+        def _(q=q):
+            wo_z(q, 1).wait_send()
+            wo_z(q, 2).wait_send()
+
+    def drain(h, carry):
+        for tau in range(2):
+            for up in range(2):
+                y_copy(tau, h, up).wait_send()
+            for dh in range(3):
+                sib_copy(tau, h, dh).wait_send()
+        for dh in range(3):
+            x_copy(h, dh).wait_send()
+        return carry
+
+    lax.fori_loop(0, 3, drain, 0)
 
     wo_ready(1)
     o_sib.append(same(wo.at[:, :, c, wrap(y + 2)], sib))
@@ -442,50 +469,20 @@
                 out0[f, i, :, a * 768 : a * 768 + 768] = r[at : at + 48]
                 out1[f, i, :, a * 768 : a * 768 + 768] = r[T + at : T + at + 48]
 
-    for cp in started + wy:
+    for cp in started[drained:] + wy:
         cp.wait_send()
-
-    for q in range(2):
-        for zz in range(2):
-            wo_pair(wz.at[q, zz], me2, q, zz).wait_send()
-
-            @pl.when(holder)
-            def _(q=q, zz=zz):
-                wo_next(q, zz).wait_send()
-
-        @pl.when(holder)
-        def _(q=q):
-            wo_z(q, 0).wait_send()
-
-        @pl.when(jnp.logical_not(holder))
-        def _(q=q):
-            wo_z(q, 1).wait_send()
-            wo_z(q, 2).wait_send()
-
-    def drain(h, carry):
-        for tau in range(2):
-            for up in range(2):
-                y_copy(tau, h, up).wait_send()
-            for dh in range(3):
-                sib_copy(tau, h, dh).wait_send()
-        for dh in range(3):
-            x_copy(h, dh).wait_send()
-        own, remote = hid_copies(zl, h)
-        for cp in remote:
+    for h in range(3):
+        for cp in hid_copies(zl, h)[1]:
             cp.wait_send()
-        return carry
-
-    lax.fori_loop(0, 3, drain, 0)
 
 
 def per_device(tokens, tangent, qkv_weight, out_weight, reach):
     any_spec = pl.BlockSpec(memory_space=pl.ANY)
     vmem = pl.BlockSpec(memory_space=pltpu.VMEM)
     dma = pltpu.SemaphoreType.DMA
-    result = jax.ShapeDtypeStruct((2, 2, 48, 1536), BF)
     return pl.pallas_call(
         kernel,
-        out_shape=(result, result),
+        out_shape=(pltpu.VMEM((2, 2, 48, 1536), BF),) * 2,
         in_specs=[pl.BlockSpec(memory_space=pltpu.SMEM)] + [any_spec] * 4,
         out_specs=(vmem, vmem),
         scratch_shapes=[

time: 93.5 us -> 84.1 us (0.90)
  Pallas kernels: 89.9 us -> 81.7 us
  local copies, waits for them, and re-layouts: 2.8 us -> 1.63 us
    pallas_call x1, Pallas kernels: 89.9 us -> 81.7 us  [per_device(): pl.pallas_call(kernel, out_shape=(pltpu.VMEM((2, 2, 48, 1536), BF),) * 2,...]
    unnamed x4 -> x2, local copies, waits for them, and re-layouts: 2.8 us -> 1.63 us
where the time goes in v3:
time: 84.1 us; the launch traced here: 84 us
  Pallas kernels  81.7 us (97%)
  local copies, waits for them, and re-layouts  1.63 us (2%)
    pallas_call x1, Pallas kernels, per_device(): pl.pallas_call(kernel, out_shape=(pltpu.VMEM((2, 2, 48, 1536), BF),) * 2,...  81.7 us

profile of v3, /device:TPU:1, one launch (start us, length us, event | category | flops | bytes accessed | tf_op | source)
XLA Modules:
  0.0 84.0 jit_solution(9324891408356341480)
XLA Ops:
  0.6 81.7 %shard_map.68 = (bf16[2,2,48,1536]{3,2,1,0:T(8,128)(2,1)S(1)}, bf16[2,2,48,1536]{3,2,1,0:T(8,128)(2,1)S(1)}) custom-call(s32[2,6]{1,0:T(2,128)} %reach.1, bf16[192,3072]{1,0:T(8,128)(2,1)} %bitcast.4, bf16[192,3072]{1,0:T(8,128)(2,1)} %bitcast.5, bf16[3,192,768]{2,1,0:T(8,128)(2,1)} %bitcast.6, bf16[192,768]{1,0:T(8,128)(2,1)} %bitcast.7), custom_call_target="tpu_custom_call" | custom-call | tf_op jit(solution)/shard_map/pallas_call | solution.py:483
  82.4 0.8 copy.9
  83.2 0.8 copy.10

commit v4 on v3

--- a/solution.py
+++ b/solution.py
@@ -10,11 +10,11 @@
 D = 3072
 QT = 48
 BF = jnp.bfloat16
-SENDS = 104
+SENDS = 106
 F32 = jnp.float32
 
 
-def kernel(reach, tok, tan, wq, wot, out0, out1, tk, wk, wqb, kv, qb, hs, hid, wz, wo, lsem, ss, rs, osem, ysem, xsem, csem, hsem):
+def kernel(reach, tok, tan, wq, wot, out0, out1, tk, wk, wqb, kv, qb, hs, hid, wz, wo, acc, lsem, ss, rs, osem, ysem, xsem, csem, hsem):
     tm = lax.axis_index("tm")
     y = lax.axis_index("height")
     mp = lax.axis_index("mp")
@@ -398,19 +398,22 @@
 
     wo_ready(0)
 
-    quarter = wo.at[:, :, c, y]
-    wy = [o_copy(quarter, quarter, d, 14 + i) for i, d in enumerate((yf, yb))]
+    def wo_y(slot, i):
+        ref = wo.at[slot, :, c, y]
+        return o_copy(ref, ref, (yf, yb)[i], 14 + 2 * slot + i)
+
+    wy = [wo_y(slot, i) for slot in range(2) for i in range(2)]
+    for cp in wy:
+        cp.start()
+    o_sib = [[same(wo.at[slot, :, c, y], sib)] for slot in range(2)]
     partner_halo(0)
     inner(0)
     partner_halo(1)
     inner(1)
     partner_halo(2)
-    for cp in wy:
-        cp.start()
     edge(0)
     inner(2)
     edge(1)
-    o_sib = [same(quarter, sib)]
     edge(2)
 
     for cp in started:
@@ -447,22 +450,31 @@
     lax.fori_loop(0, 3, drain, 0)
 
     wo_ready(1)
-    o_sib.append(same(wo.at[:, :, c, wrap(y + 2)], sib))
-    for i, cp in enumerate(wy):
-        arrived(cp)
-        o_sib.append(same(wo.at[:, :, c, wrap(y - df + 2 * df * i)], sib))
-    arrived(*o_sib)
-
-    for h in range(3):
+    for slot in range(2):
+        o_sib[slot].append(same(wo.at[slot, :, c, wrap(y + 2)], sib))
+
+    def hidden(h):
         own, remote = hid_copies(zl, h)
         own.wait()
-        for cp in remote:
-            cp.wait_recv()
-
+        arrived(*remote)
+
+    def mix(a, lo, n):
+        lhs = jnp.concatenate([hid[:, i * 384 + lo : i * 384 + lo + n] for i in range(4)], 1)
+        rhs = wo[a].reshape(768, 1536)
+        rhs = jnp.concatenate([rhs[:, i * 384 + lo : i * 384 + lo + n] for i in range(4)], 1)
+        return lax.dot_general(lhs, rhs, (((1,), (1,)), ((), ())), preferred_element_type=F32)
+
+    hidden(0)
+    hidden(1)
     for a in range(2):
-        r = lax.dot_general(
-            hid[...], wo[a].reshape(768, 1536), (((1,), (1,)), ((), ())), preferred_element_type=F32
-        ).astype(BF)
+        for i in range(2):
+            arrived(wy[2 * a + i])
+            o_sib[a].append(same(wo.at[a, :, c, wrap(y - df + 2 * df * i)], sib))
+        arrived(*o_sib[a])
+        acc[a] = mix(a, 0, 256)
+    hidden(2)
+    for a in range(2):
+        r = (acc[a] + mix(a, 256, 128)).astype(BF)
         for f in range(2):
             for i in range(2):
                 at = (2 * f + i) * 48
@@ -495,10 +507,11 @@
             pltpu.VMEM((2 * T, 1536), BF),
             pltpu.VMEM((2, 2, QT, 1536), BF),
             pltpu.VMEM((2, 2, 2, 4, QT, 1536), BF),
+            pltpu.VMEM((2, 2 * T, 768), F32),
             dma((15,)),
             dma((SENDS,)),
             dma((SENDS,)),
-            dma((2, 16)),
+            dma((2, 18)),
             dma((2, 2, 3, 2)),
             dma((2, 3, 3)),
             dma((2, 2, 3, 3)),

time: 84.1 us -> 81.7 us (0.971)
  Pallas kernels: 81.7 us -> 78.7 us
    pallas_call x1, Pallas kernels: 81.7 us -> 78.7 us  [per_device(): pl.pallas_call(kernel, out_shape=(pltpu.VMEM((2, 2, 48, 1536), BF),) * 2,...]
where the time goes in v4:
time: 81.7 us; the launch traced here: 81 us
  Pallas kernels  78.7 us (96%)
  local copies, waits for them, and re-layouts  1.63 us (2%)
    pallas_call x1, Pallas kernels, per_device(): pl.pallas_call(kernel, out_shape=(pltpu.VMEM((2, 2, 48, 1536), BF),) * 2,...  78.7 us

profile of v4, /device:TPU:1, one launch (start us, length us, event | category | flops | bytes accessed | tf_op | source)
XLA Modules:
  0.0 81.0 jit_solution(11420406698778872089)
XLA Ops:
  0.6 78.7 %shard_map.68 = (bf16[2,2,48,1536]{3,2,1,0:T(8,128)(2,1)S(1)}, bf16[2,2,48,1536]{3,2,1,0:T(8,128)(2,1)S(1)}) custom-call(s32[2,6]{1,0:T(2,128)} %reach.1, bf16[192,3072]{1,0:T(8,128)(2,1)} %bitcast.4, bf16[192,3072]{1,0:T(8,128)(2,1)} %bitcast.5, bf16[3,192,768]{2,1,0:T(8,128)(2,1)} %bitcast.6, bf16[192,768]{1,0:T(8,128)(2,1)} %bitcast.7), custom_call_target="tpu_custom_call" | custom-call | tf_op jit(solution)/shard_map/pallas_call | solution.py:495
  79.3 0.8 %copy.9 = bf16[2,2,48,1536]{3,2,1,0:T(8,128)(2,1)} copy(bf16[2,2,48,1536]{3,2,1,0:T(8,128)(2,1)S(1)} %get-tuple-element.2) | data formatting | bytes 1179648
  80.2 0.8 %copy.10 = bf16[2,2,48,1536]{3,2,1,0:T(8,128)(2,1)} copy(bf16[2,2,48,1536]{3,2,1,0:T(8,128)(2,1)S(1)} %get-tuple-element.3) | data formatting | bytes 1179648

commit v5 on v4

--- a/solution.py
+++ b/solution.py
@@ -14,7 +14,7 @@
 F32 = jnp.float32
 
 
-def kernel(reach, tok, tan, wq, wot, out0, out1, tk, wk, wqb, kv, qb, hs, hid, wz, wo, acc, lsem, ss, rs, osem, ysem, xsem, csem, hsem):
+def kernel(reach, tok, tan, wq, wot, out, tk, wk, wqb, kv, qb, hs, hid, wz, wo, acc, lsem, ss, rs, osem, ysem, xsem, csem, hsem):
     tm = lax.axis_index("tm")
     y = lax.axis_index("height")
     mp = lax.axis_index("mp")
@@ -286,12 +286,12 @@
     for m in mine:
         m.wait()
     wo_first(0)
+    wo_first(1)
     own_tile(0)
     last_y(1)
     own_tile(1)
     last_y(2)
     relay_y(3)
-    wo_first(1)
     own_tile(2)
     wo_relay(0, 0)
     own_relay(3)
@@ -412,8 +412,8 @@
     inner(1)
     partner_halo(2)
     edge(0)
+    edge(1)
     inner(2)
-    edge(1)
     edge(2)
 
     for cp in started:
@@ -464,13 +464,14 @@
         rhs = jnp.concatenate([rhs[:, i * 384 + lo : i * 384 + lo + n] for i in range(4)], 1)
         return lax.dot_general(lhs, rhs, (((1,), (1,)), ((), ())), preferred_element_type=F32)
 
-    hidden(0)
-    hidden(1)
     for a in range(2):
         for i in range(2):
             arrived(wy[2 * a + i])
             o_sib[a].append(same(wo.at[a, :, c, wrap(y - df + 2 * df * i)], sib))
         arrived(*o_sib[a])
+        if a == 0:
+            hidden(0)
+            hidden(1)
         acc[a] = mix(a, 0, 256)
     hidden(2)
     for a in range(2):
@@ -478,8 +479,8 @@
         for f in range(2):
             for i in range(2):
                 at = (2 * f + i) * 48
-                out0[f, i, :, a * 768 : a * 768 + 768] = r[at : at + 48]
-                out1[f, i, :, a * 768 : a * 768 + 768] = r[T + at : T + at + 48]
+                out[0, f, i, :, a * 768 : a * 768 + 768] = r[at : at + 48]
+                out[1, f, i, :, a * 768 : a * 768 + 768] = r[T + at : T + at + 48]
 
     for cp in started[drained:] + wy:
         cp.wait_send()
@@ -492,11 +493,11 @@
     any_spec = pl.BlockSpec(memory_space=pl.ANY)
     vmem = pl.BlockSpec(memory_space=pltpu.VMEM)
     dma = pltpu.SemaphoreType.DMA
-    return pl.pallas_call(
+    both = pl.pallas_call(
         kernel,
-        out_shape=(pltpu.VMEM((2, 2, 48, 1536), BF),) * 2,
+        out_shape=pltpu.VMEM((2, 2, 2, 48, 1536), BF),
         in_specs=[pl.BlockSpec(memory_space=pltpu.SMEM)] + [any_spec] * 4,
-        out_specs=(vmem, vmem),
+        out_specs=vmem,
         scratch_shapes=[
             pltpu.VMEM((2, 2, T, D), BF),
             pltpu.VMEM((3, 2, 4, 2, 2, T, 128), BF),
@@ -521,6 +522,7 @@
             collective_id=0, has_side_effects=True, vmem_limit_bytes=60 * 1024 * 1024
         ),
     )(reach, tokens.reshape(T, D), tangent.reshape(T, D), jnp.transpose(qkv_weight, (1, 0, 2)), out_weight.T)
+    return both[0], both[1]
 
 
 def solution(mesh):

time: 81.7 us -> 80.7 us (0.988)
    unnamed x2 -> x0, local copies, waits for them, and re-layouts: 1.63 us -> none
    squeeze x0 -> x1, local copies, waits for them, and re-layouts: none -> 1.09 us  [per_device(): return (both[0], both[1])]
where the time goes in v5:
time: 80.7 us; the launch traced here: 80.4 us
  Pallas kernels  78.7 us (98%)
  local copies, waits for them, and re-layouts  1.09 us (1%)
    pallas_call x1, Pallas kernels, per_device(): pl.pallas_call(kernel, out_shape=pltpu.VMEM((2, 2, 2, 48, 1536), BF), in_...  78.7 us

profile of v5, /device:TPU:1, one launch (start us, length us, event | category | flops | bytes accessed | tf_op | source)
XLA Modules:
  0.0 80.4 jit_solution(13933687334794117112)
XLA Ops:
  0.6 78.7 %shard_map.68 = bf16[2,2,2,48,1536]{4,3,2,1,0:T(8,128)(2,1)S(1)} custom-call(s32[2,6]{1,0:T(2,128)} %reach.1, bf16[192,3072]{1,0:T(8,128)(2,1)} %bitcast.8, bf16[192,3072]{1,0:T(8,128)(2,1)} %bitcast.9, bf16[3,192,768]{2,1,0:T(8,128)(2,1)} %bitcast.10, bf16[192,768]{1,0:T(8,128)(2,1)} %bitcast.11), custom_call_target="tpu_custom_call" | custom-call | tf_op jit(solution)/shard_map/pallas_call | solution.py:496
  79.3 1.1 %slice_bitcast_fusion = (bf16[2,2,48,1536]{3,2,1,0:T(8,128)(2,1)}, bf16[2,2,48,1536]{3,2,1,0:T(8,128)(2,1)}) fusion(bf16[2,2,2,48,1536]{4,3,2,1,0:T(8,128)(2,1)S(1)} %shard_map.68), kind=kLoop, calls=%fused_computation | loop fusion | bytes 2359296 | tf_op jit(solution)/shard_map/squeeze | solution.py:525
